TPU v7x, 256 devices: a whole 4x4x8 slice. The times are simulated.
256 devices in a mesh: wide: 32 (over x_hi, z, core), depth: 8 (over y, x_lo).
Axes of the slice: x: 4 (x_hi: 2, x_lo: 2; x = x_hi * 2 + x_lo), y: 4, z: 8, core: 2. Of those that a mesh axis runs over, the one named last changes fastest.
Arguments:
- schur: float32 [32, 8, 1536, 1536], P('wide', 'depth'), as said below
- loads: float32 [32, 8, 1536, 128], P('wide', 'depth'), may hold values from -6 to 6
- face_sizes: int32 [32, 8, 6], P('wide', 'depth'), may hold values from 64 to 256, as said below
- face_dir: int32 [32, 8, 6], P('wide', 'depth'), may hold values from 0 to 5, as said below
Outputs:
- displacement: float32 [32, 8, 1536, 128], P('wide', 'depth')
- residual: float32 [32, 8, 1536, 128], P('wide', 'depth')
Inputs may be any that keep to these rules, and one draw needn't show every extreme that they name: `face_sizes`: A face slot and the neighbour's slot facing back across the same face have the same size; some slot holds 256 used unknowns and some holds 64. `face_dir`: each subdomain's six entries are 0 to 5 in some order: 0 faces the lower neighbour along wide, 1 the upper one, 2 the lower neighbour along depth, 3 the upper one, 4 and 5 the supported top and bottom surfaces. `schur`: each subdomain's matrix is symmetric and positive definite.
All inputs are finite; a program needn't handle non-finite values.
Results may differ from a plain program's by a relative error of at most 0.00017.
Values sent between devices are 32-bit elements; how exact they have to be, the bound alone decides.
A program may use at most 128 MiB of HBM per device.

v0:
```python
import jax
import jax.numpy as jnp
from jax import lax
from jax.sharding import PartitionSpec as P

ITERS = 2


OMEGA = 0.6


def from_behind(value, axis, steps):
    count = lax.axis_size(axis)
    first, last = (max(0, -steps), min(count, count - steps))
    return lax.ppermute(value, axis, [(source, source + steps) for source in range(first, last)])


def assemble(select, parts):
    facing = jnp.einsum("kd,kfr->dfr", select, parts, precision=lax.Precision.HIGHEST)
    from_lower_w = from_behind(facing[1], "wide", 1)
    from_upper_w = from_behind(facing[0], "wide", -1)
    from_lower_d = from_behind(facing[3], "depth", 1)
    from_upper_d = from_behind(facing[2], "depth", -1)
    blank = jnp.zeros_like(facing[0])
    arrived = jnp.stack(
        [from_lower_w, from_upper_w, from_lower_d, from_upper_d, blank, blank], axis=0
    )
    return parts + jnp.einsum("kd,dfr->kfr", select, arrived, precision=lax.Precision.HIGHEST)


def local(schur, loads, face_sizes, face_dir):
    matrix = schur[0, 0]
    load = loads[0, 0]
    sizes = face_sizes[0, 0]
    dirs = face_dir[0, 0]
    order_rows = matrix.shape[0]
    slot_rows = order_rows // 6
    cases = load.shape[1]
    mask = (jnp.arange(slot_rows, dtype=jnp.int32)[None, :] < sizes[:, None]).astype(jnp.float32)
    select = (dirs[:, None] == jnp.arange(6, dtype=jnp.int32)[None, :]).astype(jnp.float32)
    shaped = matrix.reshape(6, slot_rows, 6, slot_rows)
    blocks = jnp.stack([shaped[k, :, k, :] for k in range(6)], axis=0)
    first = load.reshape(6, slot_rows, cases) * mask[:, :, None]
    summed = assemble(select, blocks)
    resid = assemble(select, first)
    ident = jnp.eye(slot_rows, dtype=jnp.float32)
    summed = summed * mask[:, :, None] * mask[:, None, :] + ident * (1.0 - mask[:, :, None])
    factor = jnp.linalg.cholesky(summed)
    inverse = jax.scipy.linalg.cho_solve((factor, True), jnp.broadcast_to(ident, summed.shape))

    def partial_value(disp):
        applied = jnp.dot(matrix, disp.reshape(order_rows, cases), precision=lax.Precision.HIGHEST)
        return (load - applied).reshape(6, slot_rows, cases) * mask[:, :, None]

    disp = jnp.zeros((6, slot_rows, cases), jnp.float32)
    for step in range(ITERS):
        if step > 0:
            resid = assemble(select, partial_value(disp))
        update = jnp.einsum("kfg,kgc->kfc", inverse, resid, precision=lax.Precision.HIGHEST)
        disp = disp + OMEGA * update
    final = assemble(select, partial_value(disp))
    return (disp.reshape(1, 1, order_rows, cases), final.reshape(1, 1, order_rows, cases))


def solution(mesh):
    return jax.shard_map(
        local,
        mesh=mesh,
        in_specs=(
            P("wide", "depth", None, None),
            P("wide", "depth", None, None),
            P("wide", "depth", None),
            P("wide", "depth", None),
        ),
        out_specs=(P("wide", "depth", None, None), P("wide", "depth", None, None)),
        check_vma=False,
    )
```

profile of v0, /device:TPU:22, one launch (start us, length us, event | category | flops | bytes accessed | tf_op | source)
XLA Modules:
  0.0 515.7 jit_solution(5207471020685836534)
XLA Ops:
  0.6 12.0 %reshape_squeeze.6 = f32[6,256,6,256]{3,2,1,0:T(8,128)} reshape(f32[1,1,1536,1536]{3,2,1,0:T(8,128)} %param.4) | data formatting | bytes 18874368 | tf_op jit(solution)/shard_map/reshape;squeeze | solution.py:41
  12.6 6.3 %fusion.60 = (f32[1,256,1,256]{3,2,1,0:T(1,128)S(1)}, f32[1,256,1,256]{3,2,1,0:T(1,128)S(1)}, f32[1,256,1,256]{3,2,1,0:T(1,128)S(1)}, f32[1,256,1,256]{3,2,1,0:T...) fusion(f32[6,256,6,256]{3,2,1,0:T(8,128)} %reshape_squeeze.6), kind=kLoop, calls=%fused_computation.88 | loop fusion | bytes 3145728 | tf_op jit(solution)/shard_map/slice | solution.py:42
  24.1 2.1 copy.93
  26.3 1.4 fusion.42
  28.5 1.9 collective-permute-start
  30.7 1.3 fusion.20
  32.0 1.2 fusion.64
  33.1 3.9 collective-permute-start.4
  37.0 6.0 %collective-permute-start.5 = (f32[256,128]{1,0:T(8,128)}, f32[256,128]{1,0:T(8,128)S(1)}, u32[]{:S(2)}, u32[]{:S(2)}) collective-permute-start(f32[256,128]{1,0:T(8,128)} %bitcast.26), channel_id=1, source_target_pairs={{8,0},{16,8},{24,16},{32,24},{40,32},{48,40},{56,48},{64,56},{72,6... | collective-permute-start | bytes 393224 | tf_op jit(solution)/shard_map/ppermute | solution.py:15
  43.1 2.7 collective-permute-start.6
  45.7 3.2 collective-permute-start.7
  50.8 1.1 copy.116
  55.5 2.0 collective-permute-start.1
  57.6 3.5 collective-permute-start.2
  61.1 2.6 collective-permute-start.3
  64.4 2.4 stack.77
  66.9 2.7 convolution_add_fusion.2
  69.9 1.2 copy.95
  71.1 1.9 copy.96
  73.0 1.7 collective-permute-done.3
  74.7 1.9 copy.97
  76.8 4.4 stack.72
  81.2 3.1 fusion.47
  84.3 1.8 copy.98
  86.1 1.8 multiply_add_fusion
  88.6 1.2 copy-done.5
  89.8 71.0 %custom-call.20 = f32[6,128,128]{2,1,0:T(8,128)} custom-call(f32[6,128,128]{2,1,0:T(8,128)S(1)} %cholesky.122), custom_call_target="Cholesky" | custom-call | tf_op jit(solution)/shard_map/jit(cholesky)/cholesky | solution.py:48
  160.8 1.2 cholesky.117
  162.8 60.8 %custom-call.21 = f32[6,1,128,128]{2,3,1,0:T(8,128)} custom-call(f32[6,1,128,128]{3,2,1,0:T(8,128)} %select_bitcast_fusion), custom_call_target="InvertDiagBlocksLowerTriangular" | custom-call | tf_op jit(solution)/shard_map/jit(cholesky)/cholesky | solution.py:48
  223.6 1.5 constant_dynamic-update-slice_fusion.1
  225.2 1.7 convolution_subtract_fusion.2
  226.8 71.1 %custom-call.22 = f32[6,128,128]{2,1,0:T(8,128)S(1)} custom-call(f32[6,128,128]{2,1,0:T(8,128)} %convolution_subtract_fusion.2), custom_call_target="Cholesky" | custom-call | tf_op jit(solution)/shard_map/jit(cholesky)/cholesky | solution.py:48
  298.0 1.1 select_reduce_fusion
  300.3 1.7 select_select_fusion
  302.1 5.7 %while.1 = (s32[]{:T(128)}, f32[6,256,256]{2,1,0:T(8,128)S(1)}, s32[2,2]{1,0:T(2,128)S(1)}, f32[2,6,128,128]{3,2,0,1:T(8,128)}, s32[]{:T(128)}) while((s32[]{:T(128)}, f32[6,256,256]{2,1,0:T(8,128)S(1)}, s32[2,2]{1,0:T(2,128)S(1)}, f32[2,6,128,128]{3,2,0,1:T(8,128)}, s32[]{:T(128)}) %tuple.45), condition=%wide.while_cond, body=%wide.while_body.sunk | while | flops 2 | bytes 788065 | solution.py:49
  302.8 2.2 bitcast_dynamic-update-slice_fusion.8
  305.6 2.2 bitcast_dynamic-update-slice_fusion.8
  307.8 118.9 %custom-call.23 = f32[6,2,128,128]{2,3,1,0:T(8,128)S(1)} custom-call(f32[6,2,128,128]{3,2,1,0:T(8,128)} %bitcast.214), custom_call_target="InvertDiagBlocksLowerTriangular" | custom-call | tf_op jit(solution)/shard_map/jit(_cho_solve)/vmap()/triangular_solve | solution.py:49
  427.6 1.9 fusion.29
  429.5 1.8 convolution_subtract_fusion.1
  431.3 1.9 fusion.33
  436.5 1.6 convolution_multiply_fusion.1
  438.2 11.0 %fusion.7 = f32[1536,128]{0,1:T(8,128)} fusion(f32[1536,128]{1,0:T(8,128)S(1)} %bitcast.181, f32[1,1,1536,1536]{3,2,1,0:T(8,128)S(1)} %bitcast.174, f32[1,1,1536,128]{2,3,1,0:T(8,128)S(1)} %copy-done.1), kind=kOutput, calls=%fused_computation.7 | convolution fusion | flops 3624075264 | bytes 11796480 | tf_op jit(solution)/shard_map/dot_general | solution.py:52
  449.2 1.4 copy.117
  450.6 1.3 fusion.19
  452.3 1.9 collective-permute-start.8
  454.2 7.3 %collective-permute-start.9 = (f32[256,128]{1,0:T(8,128)S(1)}, f32[256,128]{1,0:T(8,128)}, u32[]{:S(2)}, u32[]{:S(2)}) collective-permute-start(f32[256,128]{1,0:T(8,128)S(1)} %bitcast.200), channel_id=1, source_target_pairs={{8,0},{16,8},{24,16},{32,24},{40,32},{48,40},{56,48},{64,56},{72,6... | collective-permute-start | bytes 393224 | tf_op jit(solution)/shard_map/ppermute | solution.py:15
  461.5 2.6 collective-permute-start.10
  464.1 3.2 collective-permute-start.11
  467.3 1.1 collective-permute-done.10
  468.4 3.5 collective-permute-done.11
  472.0 3.5 stack.82
  475.4 2.4 convolution_add_fusion.1
  477.9 1.7 fusion.17
  480.4 10.8 %fusion.13 = f32[1536,128]{0,1:T(8,128)S(1)} fusion(f32[1536,128]{1,0:T(8,128)S(1)} %bitcast.182, f32[1,1,1536,1536]{3,2,1,0:T(8,128)} %param.4, f32[1,1,1536,128]{2,3,1,0:T(8,128)S(1)} %copy-done.1), kind=kOutput, calls=%fused_computation.9 | convolution fusion | flops 3624075264 | bytes 11796480 | tf_op jit(solution)/shard_map/dot_general | solution.py:52
  491.5 1.3 fusion.18
  493.1 1.9 collective-permute-start.12
  495.1 7.3 %collective-permute-start.13 = (f32[256,128]{1,0:T(8,128)S(1)}, f32[256,128]{1,0:T(8,128)S(1)}, u32[]{:S(2)}, u32[]{:S(2)}) collective-permute-start(f32[256,128]{1,0:T(8,128)S(1)} %bitcast.201), channel_id=1, source_target_pairs={{8,0},{16,8},{24,16},{32,24},{40,32},{48,40},{56,48},{64,56},{72,6... | collective-permute-start | bytes 393224 | tf_op jit(solution)/shard_map/ppermute | solution.py:15
  502.3 2.0 collective-permute-start.14
  504.4 3.8 collective-permute-start.15
  509.2 2.9 collective-permute-done.15
  512.1 1.1 stack.87
  513.2 1.1 convolution_add_fusion
  514.3 1.0 copy.132
  (111 shorter events, 24.0 us)
Async XLA Ops:
  24.1 2.1 copy-start.18
  27.7 2.8 copy-start.20
  27.7 3.0 copy-start
  28.5 41.1 %collective-permute-start = (f32[256,256]{1,0:T(8,128)S(1)}, f32[256,256]{1,0:T(8,128)S(1)}, u32[]{:S(2)}, u32[]{:S(2)}) collective-permute-start(f32[256,256]{1,0:T(8,128)S(1)} %bitcast.185), channel_id=1, source_target_pairs={{0,8},{8,16},{16,24},{24,32},{32,40},{40,48},{48,56},{56,64},{64,7... | collective-permute-start | bytes 786440 | tf_op jit(solution)/shard_map/ppermute | solution.py:15
  33.1 22.4 %collective-permute-start.4 = (f32[256,128]{1,0:T(8,128)}, f32[256,128]{1,0:T(8,128)S(1)}, u32[]{:S(2)}, u32[]{:S(2)}) collective-permute-start(f32[256,128]{1,0:T(8,128)} %bitcast.23), channel_id=1, source_target_pairs={{0,8},{8,16},{16,24},{24,32},{32,40},{40,48},{48,56},{56,64},{64,7... | collective-permute-start | bytes 393224 | tf_op jit(solution)/shard_map/ppermute | solution.py:15
  37.0 20.5 %collective-permute-start.5 = (f32[256,128]{1,0:T(8,128)}, f32[256,128]{1,0:T(8,128)S(1)}, u32[]{:S(2)}, u32[]{:S(2)}) collective-permute-start(f32[256,128]{1,0:T(8,128)} %bitcast.26), channel_id=1, source_target_pairs={{8,0},{16,8},{24,16},{32,24},{40,32},{48,40},{56,48},{64,56},{72,6... | collective-permute-start | bytes 393224 | tf_op jit(solution)/shard_map/ppermute | solution.py:15
  43.1 18.0 %collective-permute-start.6 = (f32[256,128]{1,0:T(8,128)}, f32[256,128]{1,0:T(8,128)S(1)}, u32[]{:S(2)}, u32[]{:S(2)}) collective-permute-start(f32[256,128]{1,0:T(8,128)} %bitcast.29), channel_id=1, source_target_pairs={{0,1},{1,2},{2,3},{3,4},{4,5},{5,6},{6,7},{8,9},{9,10},{10,11},{11... | collective-permute-start | bytes 393224 | tf_op jit(solution)/shard_map/ppermute | solution.py:15
  45.7 18.0 %collective-permute-start.7 = (f32[256,128]{1,0:T(8,128)}, f32[256,128]{1,0:T(8,128)S(1)}, u32[]{:S(2)}, u32[]{:S(2)}) collective-permute-start(f32[256,128]{1,0:T(8,128)} %bitcast.32), channel_id=1, source_target_pairs={{1,0},{2,1},{3,2},{4,3},{5,4},{6,5},{7,6},{9,8},{10,9},{11,10},{12... | collective-permute-start | bytes 393224 | tf_op jit(solution)/shard_map/ppermute | solution.py:15
  55.5 14.3 %collective-permute-start.1 = (f32[256,256]{1,0:T(8,128)S(1)}, f32[256,256]{1,0:T(8,128)}, u32[]{:S(2)}, u32[]{:S(2)}) collective-permute-start(f32[256,256]{1,0:T(8,128)S(1)} %bitcast.187), channel_id=1, source_target_pairs={{8,0},{16,8},{24,16},{32,24},{40,32},{48,40},{56,48},{64,56},{72,6... | collective-permute-start | bytes 786440 | tf_op jit(solution)/shard_map/ppermute | solution.py:15
  57.6 13.5 %collective-permute-start.2 = (f32[256,256]{1,0:T(8,128)}, f32[256,256]{1,0:T(8,128)}, u32[]{:S(2)}, u32[]{:S(2)}) collective-permute-start(f32[256,256]{1,0:T(8,128)} %bitcast.164), channel_id=1, source_target_pairs={{0,1},{1,2},{2,3},{3,4},{4,5},{5,6},{6,7},{8,9},{9,10},{10,11},{11... | collective-permute-start | bytes 786440 | tf_op jit(solution)/shard_map/ppermute | solution.py:15
  61.1 2.7 copy-start.14
  61.1 13.7 %collective-permute-start.3 = (f32[256,256]{1,0:T(8,128)}, f32[256,256]{1,0:T(8,128)}, u32[]{:S(2)}, u32[]{:S(2)}) collective-permute-start(f32[256,256]{1,0:T(8,128)} %bitcast.163), channel_id=1, source_target_pairs={{1,0},{2,1},{3,2},{4,3},{5,4},{6,5},{7,6},{9,8},{10,9},{11,10},{12... | collective-permute-start | bytes 786440 | tf_op jit(solution)/shard_map/ppermute | solution.py:15
  63.7 0.7 copy-start.15
  64.4 5.1 copy-start.7
  88.6 1.2 copy-start.5
  89.8 72.2 %copy-start.17 = (pred[128,128]{1,0:T(8,128)(4,1)S(1)}, pred[128,128]{1,0:T(8,128)(4,1)}, u32[]{:S(2)}) copy-start(pred[128,128]{1,0:T(8,128)(4,1)} %iota_compare_fusion.2) | copy-start | bytes 49156
  89.8 133.8 %copy-start.6 = (f32[6,256,256]{2,1,0:T(8,128)S(1)}, f32[6,256,256]{2,1,0:T(8,128)}, u32[]{:S(2)}) copy-start(f32[6,256,256]{2,1,0:T(8,128)} %copy-done.5) | copy-start | bytes 4718596
  160.8 1.2 copy-start.9
  223.6 74.4 %copy-start.16 = (pred[128,128]{1,0:T(8,128)(4,1)S(1)}, pred[128,128]{1,0:T(8,128)(4,1)}, u32[]{:S(2)}) copy-start(pred[128,128]{1,0:T(8,128)(4,1)} %iota_compare_fusion.3) | copy-start | bytes 49156
  299.1 1.2 copy-start.4
  300.2 1.8 copy-start.21
  300.2 137.9 %slice-start = ((s8[9437184]{0:T(1024)(128)(4,1)}), s8[1048576]{0:T(1024)(128)(4,1)S(1)}, s32[]{:S(2)}) async-start(s8[9437184]{0:T(1024)(128)(4,1)} %bitcast.173), calls=%async_computation | async-start | bytes 2097152
  426.7 0.9 copy-start.12
  427.6 10.6 %slice-start.1 = ((s8[9437184]{0:T(1024)(128)(4,1)}), s8[4194304]{0:T(1024)(128)(4,1)S(1)}, s32[]{:S(2)}) async-start(s8[9437184]{0:T(1024)(128)(4,1)} %bitcast.173), calls=%async_computation.1 | async-start | bytes 8388608
  429.5 3.7 copy-start.13
  433.1 3.4 copy-start.10
  434.0 4.2 slice-start.2
  435.6 0.9 copy-start.2
  436.5 1.6 copy-start.1
  449.2 1.4 copy-start.19
  450.6 21.4 %copy-start.8 = (f32[2,256,128]{2,0,1:T(2,128)S(1)}, f32[2,256,128]{2,0,1:T(2,128)}, u32[]{:S(2)}) copy-start(f32[2,256,128]{2,0,1:T(2,128)} %copy-done.7) | copy-start | bytes 786436
  452.3 15.1 %collective-permute-start.8 = (f32[256,128]{1,0:T(8,128)S(1)}, f32[256,128]{1,0:T(8,128)}, u32[]{:S(2)}, u32[]{:S(2)}) collective-permute-start(f32[256,128]{1,0:T(8,128)S(1)} %bitcast.202), channel_id=1, source_target_pairs={{0,8},{8,16},{16,24},{24,32},{32,40},{40,48},{48,56},{56,64},{64,7... | collective-permute-start | bytes 393224 | tf_op jit(solution)/shard_map/ppermute | solution.py:15
  454.2 13.1 %collective-permute-start.9 = (f32[256,128]{1,0:T(8,128)S(1)}, f32[256,128]{1,0:T(8,128)}, u32[]{:S(2)}, u32[]{:S(2)}) collective-permute-start(f32[256,128]{1,0:T(8,128)S(1)} %bitcast.200), channel_id=1, source_target_pairs={{8,0},{16,8},{24,16},{32,24},{40,32},{48,40},{56,48},{64,56},{72,6... | collective-permute-start | bytes 393224 | tf_op jit(solution)/shard_map/ppermute | solution.py:15
  461.5 7.0 %collective-permute-start.10 = (f32[256,128]{1,0:T(8,128)S(1)}, f32[256,128]{1,0:T(8,128)}, u32[]{:S(2)}, u32[]{:S(2)}) collective-permute-start(f32[256,128]{1,0:T(8,128)S(1)} %bitcast.198), channel_id=1, source_target_pairs={{0,1},{1,2},{2,3},{3,4},{4,5},{5,6},{6,7},{8,9},{9,10},{10,11},{11... | collective-permute-start | bytes 393224 | tf_op jit(solution)/shard_map/ppermute | solution.py:15
  464.1 7.9 %collective-permute-start.11 = (f32[256,128]{1,0:T(8,128)S(1)}, f32[256,128]{1,0:T(8,128)}, u32[]{:S(2)}, u32[]{:S(2)}) collective-permute-start(f32[256,128]{1,0:T(8,128)S(1)} %bitcast.196), channel_id=1, source_target_pairs={{1,0},{2,1},{3,2},{4,3},{5,4},{6,5},{7,6},{9,8},{10,9},{11,10},{12... | collective-permute-start | bytes 393224 | tf_op jit(solution)/shard_map/ppermute | solution.py:15
  475.4 2.4 copy-start.3
  479.5 0.9 copy-start.11
  493.1 15.1 %collective-permute-start.12 = (f32[256,128]{1,0:T(8,128)S(1)}, f32[256,128]{1,0:T(8,128)S(1)}, u32[]{:S(2)}, u32[]{:S(2)}) collective-permute-start(f32[256,128]{1,0:T(8,128)S(1)} %bitcast.203), channel_id=1, source_target_pairs={{0,8},{8,16},{16,24},{24,32},{32,40},{40,48},{48,56},{56,64},{64,7... | collective-permute-start | bytes 393224 | tf_op jit(solution)/shard_map/ppermute | solution.py:15
  495.1 13.1 %collective-permute-start.13 = (f32[256,128]{1,0:T(8,128)S(1)}, f32[256,128]{1,0:T(8,128)S(1)}, u32[]{:S(2)}, u32[]{:S(2)}) collective-permute-start(f32[256,128]{1,0:T(8,128)S(1)} %bitcast.201), channel_id=1, source_target_pairs={{8,0},{16,8},{24,16},{32,24},{40,32},{48,40},{56,48},{64,56},{72,6... | collective-permute-start | bytes 393224 | tf_op jit(solution)/shard_map/ppermute | solution.py:15
  502.3 6.9 %collective-permute-start.14 = (f32[256,128]{1,0:T(8,128)S(1)}, f32[256,128]{1,0:T(8,128)S(1)}, u32[]{:S(2)}, u32[]{:S(2)}) collective-permute-start(f32[256,128]{1,0:T(8,128)S(1)} %bitcast.199), channel_id=1, source_target_pairs={{0,1},{1,2},{2,3},{3,4},{4,5},{5,6},{6,7},{8,9},{9,10},{10,11},{11... | collective-permute-start | bytes 393224 | tf_op jit(solution)/shard_map/ppermute | solution.py:15
  504.4 7.8 %collective-permute-start.15 = (f32[256,128]{1,0:T(8,128)S(1)}, f32[256,128]{1,0:T(8,128)S(1)}, u32[]{:S(2)}, u32[]{:S(2)}) collective-permute-start(f32[256,128]{1,0:T(8,128)S(1)} %bitcast.197), channel_id=1, source_target_pairs={{1,0},{2,1},{3,2},{4,3},{5,4},{6,5},{7,6},{9,8},{10,9},{11,10},{12... | collective-permute-start | bytes 393224 | tf_op jit(solution)/shard_map/ppermute | solution.py:15
where the time goes:
time: 526 us; the launch traced here: 516 us
  other arithmetic  330 us (63%)
  local copies, waits for them, and re-layouts  66.8 us (13%)
  starting transfers between devices  55.9 us (11%)
  matrix products  50.8 us (10%)
  waiting for transfers between devices  10.2 us (2%)
    another operation x9, other arithmetic, local(): factor = jnp.linalg.cholesky(summed)  206 us
    another operation x4, other arithmetic, local(): jax.scipy.linalg.cho_solve((factor, True), jnp.broadcast_to(ident, summed...  122 us
    ppermute x16, starting transfers between devices, from_behind(): lax.ppermute(value, axis, [(source, source + steps) for source in range(f...  55.9 us
    dot_general x2, matrix products, partial_value(): jnp.dot(matrix, disp.reshape(order_rows, cases), precision=lax.Precision....  21.8 us
    another operation x9, local copies, waits for them, and re-layouts, assemble(): jnp.stack([from_lower_w, from_upper_w, from_lower_d, from_upper_d, blank,...  16.7 us
    unnamed x66, local copies, waits for them, and re-layouts  12.6 us
    another operation x1, local copies, waits for them, and re-layouts, local(): shaped = matrix.reshape(6, slot_rows, 6, slot_rows)  12 us
  transfers between devices with their start and end apart: 16, of which 5 were waited for; matrix products, arithmetic and copies ran while one was open for 3% of the time, Pallas kernels for 0%

commit v1 on v0

v1 whole, which is shorter than its diff:
```python
import functools

import jax
import jax.numpy as jnp
from jax import lax
from jax.experimental import pallas as pl
from jax.experimental.pallas import tpu as pltpu
from jax.sharding import PartitionSpec as P

OMEGA = 0.6
MESH = pl.DeviceIdType.MESH
F32 = jnp.float32
BF16 = jnp.bfloat16

ORDER = (2, 3, 0, 1, 4, 5)
FACES = 6
ROWS = 256
HALF = 128
BLOCK = 32


def split(x):
    high = x.astype(BF16)
    return high, (x - high.astype(F32)).astype(BF16)


def mm(a, b):
    ah, al = split(a)
    bh, bl = split(b)
    w = jnp.concatenate([bh, bl], 1)
    o = jnp.dot(jnp.concatenate([ah, al], 1), jnp.concatenate([w, w], 0), preferred_element_type=F32)
    return o[:, :HALF] + o[:, HALF:]


def row(x, i):
    return jnp.broadcast_to(x[i:i + 1], (8, HALF))


def packed_inverse(groups):
    tiles = BLOCK // 8
    lane = lax.broadcasted_iota(jnp.int32, (8, HALF), 1)
    sub = lax.broadcasted_iota(jnp.int32, (8, HALF), 0)
    seg = lane & 96
    within = lane & 31
    parts = [[g[8 * t:8 * t + 8] for t in range(tiles)] for g in groups]
    for m in range(tiles):
        inside = (within >> 3) == m
        cols = []
        for part in parts:
            cols.append([[jnp.take_along_axis(x, seg + (8 * m + k), axis=1) for x in part] for k in range(8)])
            for t in range(tiles):
                ident = (within == sub + 8 * t).astype(F32)
                part[t] = jnp.where(inside, ident, part[t])
        for i in range(8):
            here = sub == i
            for part, c in zip(parts, cols):
                rp = 1.0 / row(c[i][m], i)
                rn = row(part[m], i) * rp
                for k in range(i + 1, 8):
                    f = row(c[k][m], i) * rp
                    for t in range(tiles):
                        u = c[k][t] - c[i][t] * f
                        c[k][t] = jnp.where(here, f, u) if t == m else u
                for t in range(tiles):
                    u = part[t] - c[i][t] * rn
                    part[t] = jnp.where(here, rn, u) if t == m else u
    return [jnp.concatenate(part, 0) for part in parts]


def invert_halves(ref):
    count = ref.shape[0]
    groups = [list(range(g, min(g + 4, count))) for g in range(0, count, 4)]

    def body(s, carry):
        lane = lax.broadcasted_iota(jnp.int32, (BLOCK, HALF), 1)
        lanes = lax.broadcasted_iota(jnp.int32, (HALF, HALF), 1)
        sub = lax.broadcasted_iota(jnp.int32, (BLOCK, HALF), 0)
        here = pl.ds(pl.multiple_of(s * BLOCK, BLOCK), BLOCK)
        ident = ((lane & 31) == sub).astype(F32)
        packs, panels = [], []
        for group in groups:
            pack, panel = ident, []
            for i in group:
                active = (lane >> 5) == ((i + s) & 3)
                r = ref[i, here, :]
                pack = jnp.where(active, r, pack)
                panel.append(jnp.where(active, ident, r))
            packs.append(pack)
            panels.append(panel)
        inverses = packed_inverse(packs)
        for group, inverse, panel in zip(groups, inverses, panels):

            def by_segment(blocks):
                out = []
                for b in range(4):
                    x = jnp.zeros((BLOCK, HALF), F32)
                    for block, i in zip(blocks, group):
                        x = jnp.where(((i + s) & 3) == b, block, x)
                    out.append(x)
                return jnp.concatenate(out, 0)

            left = jnp.concatenate([jnp.where((lane >> 5) == ((i + s) & 3), inverse, 0.0) for i in group], 0)
            rn = mm(left, by_segment(panel))
            rns = [rn[BLOCK * x:BLOCK * x + BLOCK] for x in range(len(group))]
            cs, rests = [], []
            for i in group:
                active = (lanes >> 5) == ((i + s) & 3)
                m = ref[i]
                cs.append(jnp.where(active, m, 0.0))
                rests.append(jnp.where(active, 0.0, m))
            o = mm(jnp.concatenate(cs, 0), by_segment(rns))
            for x, i in enumerate(group):
                ref[i] = rests[x] - o[HALF * x:HALF * x + HALF]
                ref[i, here, :] = rns[x]
        return carry

    lax.fori_loop(0, HALF // BLOCK, body, 0)


def rotate(x, i):
    return x if i % 4 == 0 else pltpu.roll(x, BLOCK * (i % 4), 1)


def kernel(grid, schur, loads, sizes, dirs, disp_out, resid_out,
           full, diag, load, piece, got_piece, load_send, got_load, face, got_face, sh, sl, top, low, cross,
           ih, il, u, uu, acc, out_disp, out_resid,
           dma, full_s, piece_s, piece_r, load_s, load_r, face_s, face_r):
    wide, depth = lax.axis_index("wide"), lax.axis_index("depth")
    exists = (depth > 0, depth < grid[1] - 1, wide > 0, wide < grid[0] - 1)
    device = ((wide, depth - 1), (wide, depth + 1), (wide - 1, depth), (wide + 1, depth))

    fetch_diag = []
    for k in range(FACES):
        fetch_diag.append(pltpu.make_async_copy(
            schur.at[0, 0, pl.ds(k * ROWS, ROWS), pl.ds(k * ROWS, ROWS)], diag.at[k], dma.at[k]))
        fetch_diag[-1].start()
    fetch_load = []
    for k in range(FACES):
        fetch_load.append(pltpu.make_async_copy(
            loads.at[0, 0, pl.ds(k * ROWS, ROWS), :], load.at[k], dma.at[6 + k]))
        fetch_load[-1].start()
    fetch_full = []
    for k in range(FACES):
        for e in range(FACES):
            fetch_full.append(pltpu.make_async_copy(
                schur.at[0, 0, pl.ds(k * ROWS, ROWS), pl.ds(e * ROWS, ROWS)], full.at[k, e], full_s.at[k, e]))
            fetch_full[-1].start()

    barrier = pltpu.get_barrier_semaphore()
    for i in range(4):
        @pl.when(exists[i])
        def _(i=i):
            pl.semaphore_signal(barrier, inc=1, device_id=device[i], device_id_type=MESH)

    def slot_of(direction):
        k = jnp.int32(0)
        for x in range(1, FACES):
            k = jnp.where(dirs[0, 0, x] == direction, jnp.int32(x), k)
        return k

    slot = [slot_of(d) for d in ORDER]
    size = []
    for d in ORDER:
        n = sizes[0, 0, 0]
        for x in range(1, FACES):
            n = jnp.where(dirs[0, 0, x] == d, sizes[0, 0, x], n)
        size.append(n)

    def remote(buffer, into, send, recv, i, index):
        return pltpu.make_async_remote_copy(
            src_ref=buffer.at[(*index, i)], dst_ref=into.at[(*index, i ^ 1)],
            send_sem=send.at[(*index, i)], recv_sem=recv.at[(*index, i ^ 1)],
            device_id=device[i], device_id_type=MESH)

    def start(buffer, into, send, recv, i, index):
        @pl.when(exists[i])
        def _():
            remote(buffer, into, send, recv, i, index).start()

    def arrived(buffer, into, send, recv, i, index):
        @pl.when(exists[i])
        def _():
            pltpu.make_async_remote_copy(
                src_ref=buffer.at[(*index, i)], dst_ref=into.at[(*index, i)],
                send_sem=send.at[(*index, i)], recv_sem=recv.at[(*index, i)],
                device_id=device[i], device_id_type=MESH).wait_recv()

    def sent(buffer, into, send, recv, i, index):
        @pl.when(exists[i])
        def _():
            remote(buffer, into, send, recv, i, index).wait_send()

    pieces = (piece, got_piece, piece_s, piece_r)
    firsts = (load_send, got_load, load_s, load_r)
    faces = (face, got_face, face_s, face_r)

    for i in range(4):
        @pl.when(jnp.logical_not(exists[i]))
        def _(i=i):
            for j in range(3):
                got_piece[j, i] = jnp.zeros((HALF, HALF), F32)
            got_load[i] = jnp.zeros((ROWS, HALF), F32)
            for j in range(2):
                got_face[j, i] = jnp.zeros((ROWS, HALF), F32)

    for c in fetch_diag:
        c.wait()
    parts = ((0, 0), (HALF, 0), (HALF, HALF))
    for i in range(4):
        for j, (r, c) in enumerate(parts):
            piece[j, i] = diag[slot[i], pl.ds(r, HALF), pl.ds(c, HALF)]

    count = jnp.int32(0)
    for e in exists:
        count = count + jnp.where(e, jnp.int32(1), jnp.int32(0))
    pl.semaphore_wait(barrier, count)
    for j in range(3):
        for i in range(4):
            start(*pieces, i, (j,))
    for c in fetch_load:
        c.wait()
    rowid = lax.broadcasted_iota(jnp.int32, (ROWS, HALF), 0)

    def masked(x, i):
        return jnp.where(rowid < size[i], x, 0.0)

    for i in range(FACES):
        x = masked(load[slot[i]], i)
        acc[i] = x
        if i < 4:
            load_send[i] = x
    for i in range(4):
        start(*firsts, i, ())

    for c in fetch_full:
        c.wait()
    for i in range(FACES):
        for e in range(FACES):
            x = full[slot[i], slot[e]]
            h, l = split(x)
            sh[pl.ds(i * ROWS, ROWS), pl.ds(e * ROWS, ROWS)] = h
            sl[pl.ds(i * ROWS, ROWS), pl.ds(e * ROWS, ROWS)] = l

    hr = lax.broadcasted_iota(jnp.int32, (HALF, HALF), 0)
    hc = lax.broadcasted_iota(jnp.int32, (HALF, HALF), 1)

    def assembled(j, i):
        r, c = parts[j]
        x = diag[slot[i], pl.ds(r, HALF), pl.ds(c, HALF)]
        if i < 4:
            arrived(*pieces, i, (j,))
            x = x + got_piece[j, i]
        x = jnp.where((hr + r < size[i]) & (hc + c < size[i]), x, 0.0)
        if r == c:
            x = jnp.where((hr == hc) & (hr + r >= size[i]), 1.0, x)
        return x

    for i in range(FACES):
        top[i] = rotate(assembled(0, i), i)
    invert_halves(top)
    for i in range(FACES):
        p = rotate(top[i], -i)
        top[i] = p
        b = assembled(1, i)
        w = mm(b, p)
        cross[i] = w
        low[i] = rotate(assembled(2, i) - mm(w, b.T), i)
    invert_halves(low)
    for i in range(FACES):
        w = cross[i]
        q = rotate(low[i], -i)
        v = -mm(q, w)
        for r, c, x in ((0, 0, top[i] - mm(w.T, v)), (HALF, 0, v), (0, HALF, v.T), (HALF, HALF, q)):
            h, l = split(x)
            ih[i, pl.ds(r, HALF), pl.ds(c, HALF)] = h
            il[i, pl.ds(r, HALF), pl.ds(c, HALF)] = l

    def solve(i, r):
        h, l = split(r)
        w = jnp.concatenate([h, l], 1)
        o = jnp.dot(ih[i], w, preferred_element_type=F32) + jnp.dot(il[i], w, preferred_element_type=F32)
        return OMEGA * (o[:, :HALF] + o[:, HALF:])

    def keep(i, x):
        u[i] = x
        h, l = split(x)
        uu[pl.ds(i * ROWS, ROWS), pl.ds(0, HALF)] = h
        uu[pl.ds(i * ROWS, ROWS), pl.ds(HALF, HALF)] = l

    def applied(i, begin, end):
        rows, cols = pl.ds(i * ROWS, ROWS), pl.ds(begin * ROWS, (end - begin) * ROWS)
        w = uu[cols, :]
        o = jnp.dot(sh[rows, cols], w, preferred_element_type=F32) + jnp.dot(sl[rows, cols], w, preferred_element_type=F32)
        return o[:, :HALF] + o[:, HALF:]

    for i in range(FACES):
        r = acc[i]
        if i < 4:
            arrived(*firsts, i, ())
            r = r + got_load[i]
        keep(i, solve(i, r))
    for i in range(FACES):
        x = acc[i] - masked(applied(i, 0, FACES), i)
        face[0, i] = x
        if i < 4:
            start(*faces, i, (0,))

    for i in (4, 5, 2, 3):
        r = face[0, i]
        if i < 4:
            arrived(*faces, i, (0,))
            r = r + got_face[0, i]
        keep(i, u[i] + solve(i, r))
    for i in range(FACES):
        acc[i] = acc[i] - masked(applied(i, 2, FACES), i)
    for i in (0, 1):
        arrived(*faces, i, (0,))
        keep(i, u[i] + solve(i, face[0, i] + got_face[0, i]))
    for i in range(FACES):
        x = acc[i] - masked(applied(i, 0, 2), i)
        face[1, i] = x
        if i < 4:
            start(*faces, i, (1,))

    def place(k):
        d = dirs[0, 0, k]
        return jnp.where(d < 2, d + 2, jnp.where(d < 4, d - 2, d))

    for k in range(FACES):
        out_disp[pl.ds(k * ROWS, ROWS), :] = u[place(k)]
    give_disp = pltpu.make_async_copy(out_disp, disp_out.at[0, 0], dma.at[12])
    give_disp.start()
    for i in (4, 5, 2, 3, 0, 1):
        x = face[1, i]
        if i < 4:
            arrived(*faces, i, (1,))
            x = x + got_face[1, i]
        acc[i] = x
    for k in range(FACES):
        out_resid[pl.ds(k * ROWS, ROWS), :] = acc[place(k)]
    give_resid = pltpu.make_async_copy(out_resid, resid_out.at[0, 0], dma.at[13])
    give_resid.start()
    for i in range(4):
        for j in range(3):
            sent(*pieces, i, (j,))
        sent(*firsts, i, ())
        for j in range(2):
            sent(*faces, i, (j,))
    give_disp.wait()
    give_resid.wait()


def solution(mesh):
    grid = (mesh.shape["wide"], mesh.shape["depth"])

    def local(schur, loads, face_sizes, face_dir):
        order, cases = schur.shape[2], loads.shape[3]
        shape = jax.ShapeDtypeStruct((1, 1, order, cases), F32)
        hbm = pl.BlockSpec(memory_space=pl.ANY)
        smem = pl.BlockSpec(memory_space=pltpu.SMEM)
        vmem = pltpu.VMEM
        sem = pltpu.SemaphoreType.DMA
        return pl.pallas_call(
            functools.partial(kernel, grid),
            out_shape=(shape, shape),
            in_specs=[hbm, hbm, smem, smem],
            out_specs=(hbm, hbm),
            scratch_shapes=[
                vmem((FACES, FACES, ROWS, ROWS), F32),
                vmem((FACES, ROWS, ROWS), F32),
                vmem((FACES, ROWS, HALF), F32),
                vmem((3, 4, HALF, HALF), F32),
                vmem((3, 4, HALF, HALF), F32),
                vmem((4, ROWS, HALF), F32),
                vmem((4, ROWS, HALF), F32),
                vmem((2, FACES, ROWS, HALF), F32),
                vmem((2, 4, ROWS, HALF), F32),
                vmem((order, order), BF16),
                vmem((order, order), BF16),
                vmem((FACES, HALF, HALF), F32),
                vmem((FACES, HALF, HALF), F32),
                vmem((FACES, HALF, HALF), F32),
                vmem((FACES, ROWS, ROWS), BF16),
                vmem((FACES, ROWS, ROWS), BF16),
                vmem((FACES, ROWS, HALF), F32),
                vmem((order, ROWS), BF16),
                vmem((FACES, ROWS, HALF), F32),
                vmem((order, cases), F32),
                vmem((order, cases), F32),
                sem((14,)),
                sem((FACES, FACES)),
                sem((3, 4)),
                sem((3, 4)),
                sem((4,)),
                sem((4,)),
                sem((2, 4)),
                sem((2, 4)),
            ],
            compiler_params=pltpu.CompilerParams(
                collective_id=0, has_side_effects=True, vmem_limit_bytes=56 << 20),
        )(schur, loads, face_sizes, face_dir)

    return jax.shard_map(
        local,
        mesh=mesh,
        in_specs=(
            P("wide", "depth", None, None),
            P("wide", "depth", None, None),
            P("wide", "depth", None),
            P("wide", "depth", None),
        ),
        out_specs=(P("wide", "depth", None, None), P("wide", "depth", None, None)),
        check_vma=False,
    )
```

time: 526 us -> 56.7 us (0.11)
  the two profiles are of different devices: /device:TPU:22 before, /device:TPU:253 now
where the time goes in v1:
time: 56.7 us; the launch traced here: 56.6 us
  Pallas kernels  51.8 us (91%)
  local copies, waits for them, and re-layouts  4.13 us (7%)
  between operations  0.64 us (1%)
    pallas_call x1, Pallas kernels, local(): pl.pallas_call(functools.partial(kernel, grid), out_shape=(shape, shape),...  51.8 us
    unnamed x2, local copies, waits for them, and re-layouts  4.13 us

profile of v1, /device:TPU:253, one launch (start us, length us, event | category | flops | bytes accessed | tf_op | source)
XLA Modules:
  0.0 56.6 jit_solution(4777787087409382840)
XLA Ops:
  0.6 51.8 %shard_map.59 = (f32[1,1,1536,128]{3,2,1,0:T(8,128)}, f32[1,1,1536,128]{3,2,1,0:T(8,128)}) custom-call(f32[1,1,1536,1536]{3,2,1,0:T(8,128)} %schur.1, f32[1,1,1536,128]{3,2,1,0:T(8,128)} %loads.1, s32[1,1,6]{2,1,0:T(1,128)} %sizes.1, s32[1,1,6]{2,1,0:T(1,128)} %dirs.1), custom_call_target="tpu_custom_call" | custom-call | tf_op jit(solution)/shard_map/pallas_call | solution.py:363
  52.4 2.1 %copy.8 = f32[1,1,1536,128]{3,2,1,0:T(8,128)} copy(f32[1,1,1536,128]{3,2,1,0:T(8,128)} %get-tuple-element.4) | data formatting | bytes 1572864
  54.5 2.1 %copy.9 = f32[1,1,1536,128]{3,2,1,0:T(8,128)} copy(f32[1,1,1536,128]{3,2,1,0:T(8,128)} %get-tuple-element.5) | data formatting | bytes 1572864

commit v2 on v1

v2 whole, which is shorter than its diff:
```python
import functools

import jax
import jax.numpy as jnp
from jax import lax
from jax.experimental import pallas as pl
from jax.experimental.pallas import tpu as pltpu
from jax.sharding import PartitionSpec as P

OMEGA = 0.6
MESH = pl.DeviceIdType.MESH
F32 = jnp.float32
BF16 = jnp.bfloat16

ORDER = (2, 3, 0, 1, 4, 5)
FACES = 6
ROWS = 256
HALF = 128
BLOCK = 32


def split(x):
    high = x.astype(BF16)
    return high, (x - high.astype(F32)).astype(BF16)


def mm(a, b):
    ah, al = split(a)
    bh, bl = split(b)
    w = jnp.concatenate([bh, bl], 1)
    o = jnp.dot(jnp.concatenate([ah, al], 1), jnp.concatenate([w, w], 0), preferred_element_type=F32)
    return o[:, :HALF] + o[:, HALF:]


def row(x, i):
    return jnp.broadcast_to(x[i:i + 1], (8, HALF))


def packed_inverse(groups):
    tiles = BLOCK // 8
    lane = lax.broadcasted_iota(jnp.int32, (8, HALF), 1)
    sub = lax.broadcasted_iota(jnp.int32, (8, HALF), 0)
    seg = lane & 96
    within = lane & 31
    parts = [[g[8 * t:8 * t + 8] for t in range(tiles)] for g in groups]
    for m in range(tiles):
        inside = (within >> 3) == m
        cols = []
        for part in parts:
            cols.append([[jnp.take_along_axis(x, seg + (8 * m + k), axis=1) for x in part] for k in range(8)])
            for t in range(tiles):
                ident = (within == sub + 8 * t).astype(F32)
                part[t] = jnp.where(inside, ident, part[t])
        for i in range(8):
            here = sub == i
            for part, c in zip(parts, cols):
                rp = 1.0 / row(c[i][m], i)
                rn = row(part[m], i) * rp
                for k in range(i + 1, 8):
                    f = row(c[k][m], i) * rp
                    for t in range(tiles):
                        u = c[k][t] - c[i][t] * f
                        c[k][t] = jnp.where(here, f, u) if t == m else u
                for t in range(tiles):
                    u = part[t] - c[i][t] * rn
                    part[t] = jnp.where(here, rn, u) if t == m else u
    return [jnp.concatenate(part, 0) for part in parts]


def invert_halves(refs, beside=None):
    def body(s, carry):
        lane = lax.broadcasted_iota(jnp.int32, (BLOCK, HALF), 1)
        lanes = lax.broadcasted_iota(jnp.int32, (HALF, HALF), 1)
        sub = lax.broadcasted_iota(jnp.int32, (BLOCK, HALF), 0)
        here = pl.ds(pl.multiple_of(s * BLOCK, BLOCK), BLOCK)
        ident = ((lane & 31) == sub).astype(F32)
        packs = []
        for ref in refs:
            pack = ident
            for i in range(ref.shape[0]):
                pack = jnp.where((lane >> 5) == ((i + s) & 3), ref[i, here, :], pack)
            packs.append(pack)
        inverses = [packed_inverse([p])[0] for p in packs]
        if beside is not None:
            beside(s)
        for ref, inverse in zip(refs, inverses):
            count = ref.shape[0]

            def by_segment(blocks):
                out = []
                for b in range(4):
                    x = jnp.zeros((BLOCK, HALF), F32)
                    for i, block in enumerate(blocks):
                        x = jnp.where(((i + s) & 3) == b, block, x)
                    out.append(x)
                return jnp.concatenate(out, 0)

            active = [(lane >> 5) == ((i + s) & 3) for i in range(count)]
            left = jnp.concatenate([jnp.where(active[i], inverse, 0.0) for i in range(count)], 0)
            rn = mm(left, by_segment([jnp.where(active[i], ident, ref[i, here, :]) for i in range(count)]))
            rns = [rn[BLOCK * i:BLOCK * i + BLOCK] for i in range(count)]
            cs, rests = [], []
            for i in range(count):
                x = ref[i]
                mine = (lanes >> 5) == ((i + s) & 3)
                cs.append(jnp.where(mine, x, 0.0))
                rests.append(jnp.where(mine, 0.0, x))
            o = mm(jnp.concatenate(cs, 0), by_segment(rns))
            for i in range(count):
                ref[i] = rests[i] - o[HALF * i:HALF * i + HALF]
                ref[i, here, :] = rns[i]
        return carry

    lax.fori_loop(0, HALF // BLOCK, body, 0)


def rotate(x, i):
    return x if i % 4 == 0 else pltpu.roll(x, BLOCK * (i % 4), 1)


def kernel(grid, schur, loads, sizes, dirs, disp_out, resid_out,
           full, diag, load, corner, got_corner, piece, got_piece, load_send, got_load, face, got_face, both, top_a, top_b, low_a, low_b, cross,
           inv, u, uu, acc, out_disp, out_resid,
           dma, full_s, disp_s, resid_s, corner_s, corner_r, piece_s, piece_r, load_s, load_r, face_s, face_r):
    top, low = (top_a, top_b), (low_a, low_b)
    wide, depth = lax.axis_index("wide"), lax.axis_index("depth")
    exists = (depth > 0, depth < grid[1] - 1, wide > 0, wide < grid[0] - 1)
    device = ((wide, depth - 1), (wide, depth + 1), (wide - 1, depth), (wide + 1, depth))

    fetch_diag = []
    for k in range(FACES):
        fetch_diag.append(pltpu.make_async_copy(
            schur.at[0, 0, pl.ds(k * ROWS, ROWS), pl.ds(k * ROWS, ROWS)], diag.at[k], dma.at[k]))
        fetch_diag[-1].start()
    fetch_load = []
    for k in range(FACES):
        fetch_load.append(pltpu.make_async_copy(
            loads.at[0, 0, pl.ds(k * ROWS, ROWS), :], load.at[k], dma.at[6 + k]))
        fetch_load[-1].start()
    fetch_full = []
    for k in range(FACES):
        for e in range(FACES):
            fetch_full.append(pltpu.make_async_copy(
                schur.at[0, 0, pl.ds(k * ROWS, ROWS), pl.ds(e * ROWS, ROWS)], full.at[k, e], full_s.at[k, e]))
            fetch_full[-1].start()

    barrier = pltpu.get_barrier_semaphore()
    for i in range(4):
        @pl.when(exists[i])
        def _(i=i):
            pl.semaphore_signal(barrier, inc=1, device_id=device[i], device_id_type=MESH)

    def slot_of(direction):
        k = jnp.int32(0)
        for x in range(1, FACES):
            k = jnp.where(dirs[0, 0, x] == direction, jnp.int32(x), k)
        return k

    slot = [slot_of(d) for d in ORDER]
    size = []
    for d in ORDER:
        n = sizes[0, 0, 0]
        for x in range(1, FACES):
            n = jnp.where(dirs[0, 0, x] == d, sizes[0, 0, x], n)
        size.append(n)

    def remote(buffer, into, send, recv, i, index):
        return pltpu.make_async_remote_copy(
            src_ref=buffer.at[(*index, i)], dst_ref=into.at[(*index, i ^ 1)],
            send_sem=send.at[(*index, i)], recv_sem=recv.at[(*index, i ^ 1)],
            device_id=device[i], device_id_type=MESH)

    def start(buffer, into, send, recv, i, index):
        @pl.when(exists[i])
        def _():
            remote(buffer, into, send, recv, i, index).start()

    def arrived(buffer, into, send, recv, i, index):
        @pl.when(exists[i])
        def _():
            pltpu.make_async_remote_copy(
                src_ref=buffer.at[(*index, i)], dst_ref=into.at[(*index, i)],
                send_sem=send.at[(*index, i)], recv_sem=recv.at[(*index, i)],
                device_id=device[i], device_id_type=MESH).wait_recv()

    def sent(buffer, into, send, recv, i, index):
        @pl.when(exists[i])
        def _():
            remote(buffer, into, send, recv, i, index).wait_send()

    corners = (corner, got_corner, corner_s, corner_r)
    pieces = (piece, got_piece, piece_s, piece_r)
    firsts = (load_send, got_load, load_s, load_r)
    faces = (face, got_face, face_s, face_r)

    for i in range(4):
        @pl.when(jnp.logical_not(exists[i]))
        def _(i=i):
            got_corner[i] = jnp.zeros((HALF + 8, HALF), F32)
            got_piece[i] = jnp.zeros((HALF, HALF), F32)
            got_load[i] = jnp.zeros((ROWS, HALF), F32)
            for j in range(2):
                got_face[j, i] = jnp.zeros((ROWS, HALF), F32)

    for c in fetch_diag:
        c.wait()
    hr = lax.broadcasted_iota(jnp.int32, (HALF, HALF), 0)
    hc = lax.broadcasted_iota(jnp.int32, (HALF, HALF), 1)
    parts = ((0, 0), (HALF, 0), (HALF, HALF))

    def own(j, i):
        r, c = parts[j]
        return diag[slot[i], pl.ds(r, HALF), pl.ds(c, HALF)]

    for i in range(4):
        first, last = own(0, i), own(2, i)
        corner[i, pl.ds(0, HALF), :] = jnp.where(hc <= hr, first, last)
        middle = jnp.sum(jnp.where(hc == hr, last, 0.0), axis=0, keepdims=True)
        corner[i, pl.ds(HALF, 8), :] = jnp.broadcast_to(middle, (8, HALF))
        piece[i] = own(1, i)

    count = jnp.int32(0)
    for e in exists:
        count = count + jnp.where(e, jnp.int32(1), jnp.int32(0))
    pl.semaphore_wait(barrier, count)
    for i in range(4):
        start(*corners, i, ())
    for c in fetch_load:
        c.wait()
    rowid = lax.broadcasted_iota(jnp.int32, (ROWS, HALF), 0)

    def masked(x, i):
        return jnp.where(rowid < size[i], x, 0.0)

    for i in range(FACES):
        x = masked(load[slot[i]], i)
        acc[i] = x
        if i < 4:
            load_send[i] = x

    def convert(half, s):
        part = ROWS // 4
        begin = pl.multiple_of(s * part, part)
        for i in range(3 * half, 3 * half + 3):
            for e in range(FACES):
                h, l = split(full[slot[i], slot[e], pl.ds(begin, part), :])
                both[pl.ds(i * 2 * ROWS + begin, part), pl.ds(e * ROWS, ROWS)] = h
                both[pl.ds(i * 2 * ROWS + ROWS + begin, part), pl.ds(e * ROWS, ROWS)] = l

    def assembled(j, i):
        r, c = parts[j]
        if i >= 4:
            x = own(j, i)
        elif j == 1:
            arrived(*pieces, i, ())
            x = piece[i] + got_piece[i]
        else:
            if j == 0:
                arrived(*corners, i, ())
            x = corner[i, pl.ds(0, HALF), :] + got_corner[i, pl.ds(0, HALF), :]
            x = jnp.where(hc <= hr if j == 0 else hc > hr, x, 0.0)
            y = x.T
            if j == 0:
                x = jnp.where(hc > hr, y, x)
            else:
                middle = corner[i, pl.ds(HALF, 8), :] + got_corner[i, pl.ds(HALF, 8), :]
                x = jnp.where(hc == hr, jnp.broadcast_to(middle[:1], (HALF, HALF)), x + y)
        x = jnp.where((hr + r < size[i]) & (hc + c < size[i]), x, 0.0)
        if r == c:
            x = jnp.where((hr == hc) & (hr + r >= size[i]), 1.0, x)
        return x

    def at(pair, i):
        return pair[i // 4].at[i % 4]

    def halve(i):
        p = rotate(at(top, i)[...], -i)
        at(top, i)[...] = p
        b = assembled(1, i)
        w = mm(b, p)
        cross[i] = w
        at(low, i)[...] = rotate(assembled(2, i) - mm(w, b.T), i)

    for c in fetch_full:
        c.wait()
    for i in (4, 5, 2, 3, 0, 1):
        at(top, i)[...] = rotate(assembled(0, i), i)
    for i in range(4):
        start(*pieces, i, ())

    for i in range(4):
        start(*firsts, i, ())

    def beside_top(s):
        convert(0, s)


    invert_halves(top, beside_top)
    for i in (4, 5, 2, 3, 0, 1):
        halve(i)
    invert_halves(low, functools.partial(convert, 1))

    def first_solve(i, r):
        p, w, q = at(top, i)[...], cross[i], rotate(at(low, i)[...], -i)
        at(low, i)[...] = q
        upper, lower = r[:HALF], r[HALF:]
        y = mm(q, lower - mm(w, upper))
        return OMEGA * jnp.concatenate([mm(p, upper) - mm(w.T, y), y], 0)

    def explicit(i):
        w, q = cross[i], at(low, i)[...]
        v = -mm(q, w)
        for r, c, x in ((0, 0, at(top, i)[...] - mm(w.T, v)), (HALF, 0, v), (0, HALF, v.T), (HALF, HALF, q)):
            h, l = split(x)
            inv[i, pl.ds(r, HALF), pl.ds(c, HALF)] = h
            inv[i, pl.ds(ROWS + r, HALF), pl.ds(c, HALF)] = l

    def folded(o):
        return (o[:ROWS, :HALF] + o[:ROWS, HALF:]) + (o[ROWS:, :HALF] + o[ROWS:, HALF:])

    def solve(i, r):
        h, l = split(r)
        w = jnp.concatenate([h, l], 1)
        return OMEGA * folded(jnp.dot(inv[i], w, preferred_element_type=F32))

    def keep(i, x):
        u[i] = x
        h, l = split(x)
        uu[pl.ds(i * ROWS, ROWS), pl.ds(0, HALF)] = h
        uu[pl.ds(i * ROWS, ROWS), pl.ds(HALF, HALF)] = l

    def applied(i, begin, end):
        rows, cols = pl.ds(i * 2 * ROWS, 4 * ROWS), pl.ds(begin * ROWS, (end - begin) * ROWS)
        o = jnp.dot(both[rows, cols], uu[cols, :], preferred_element_type=F32)
        return masked(folded(o[:2 * ROWS]), i), masked(folded(o[2 * ROWS:]), i + 1)

    for i in range(FACES):
        r = acc[i]
        if i < 4:
            arrived(*firsts, i, ())
            r = r + got_load[i]
        keep(i, first_solve(i, r))
    for i in range(0, FACES, 2):
        for j, x in enumerate(applied(i, 0, FACES)):
            face[0, i + j] = acc[i + j] - x
            if i < 4:
                start(*faces, i + j, (0,))

    for i in (4, 5, 2, 3, 0, 1):
        explicit(i)

    for i in (4, 5, 2, 3):
        r = face[0, i]
        if i < 4:
            arrived(*faces, i, (0,))
            r = r + got_face[0, i]
        keep(i, u[i] + solve(i, r))
    for i in range(0, FACES, 2):
        for j, x in enumerate(applied(i, 2, FACES)):
            acc[i + j] = acc[i + j] - x
    for i in (0, 1):
        arrived(*faces, i, (0,))
        keep(i, u[i] + solve(i, face[0, i] + got_face[0, i]))
    for i in range(0, FACES, 2):
        for j, x in enumerate(applied(i, 0, 2)):
            face[1, i + j] = acc[i + j] - x
            if i < 4:
                start(*faces, i + j, (1,))

    def place(k):
        d = dirs[0, 0, k]
        return jnp.where(d < 2, d + 2, jnp.where(d < 4, d - 2, d))

    gives = []

    def give(k, x, held, out, sems):
        rows = pl.ds(k * ROWS, ROWS)
        held[rows, :] = x
        gives.append(pltpu.make_async_copy(held.at[rows, :], out.at[0, 0, rows, :], sems.at[k]))
        gives[-1].start()

    for k in range(FACES):
        give(k, u[place(k)], out_disp, disp_out, disp_s)
    for i in (4, 5, 2, 3, 0, 1):
        x = face[1, i]
        if i < 4:
            arrived(*faces, i, (1,))
            x = x + got_face[1, i]
        acc[i] = x
    for k in range(FACES):
        give(k, acc[place(k)], out_resid, resid_out, resid_s)
    for i in range(4):
        sent(*corners, i, ())
        sent(*pieces, i, ())
        sent(*firsts, i, ())
        for j in range(2):
            sent(*faces, i, (j,))
    for c in gives:
        c.wait()


def hand_over(disp, resid, disp_out, resid_out, held, sems):
    rows = disp.shape[2] // 3
    ins, outs = [], []
    for i, (a, b) in enumerate(((disp, disp_out), (resid, resid_out))):
        for k in range(3):
            part = pl.ds(k * rows, rows)
            ins.append(pltpu.make_async_copy(a.at[0, 0, part, :], held.at[i, k], sems.at[0, i, k]))
            outs.append(pltpu.make_async_copy(held.at[i, k], b.at[0, 0, part, :], sems.at[1, i, k]))
            ins[-1].start()
    for c, d in zip(ins, outs):
        c.wait()
        d.start()
    for d in outs:
        d.wait()


def solution(mesh):
    grid = (mesh.shape["wide"], mesh.shape["depth"])

    def local(schur, loads, face_sizes, face_dir):
        order, cases = schur.shape[2], loads.shape[3]
        shape = jax.ShapeDtypeStruct((1, 1, order, cases), F32)
        hbm = pl.BlockSpec(memory_space=pl.ANY)
        smem = pl.BlockSpec(memory_space=pltpu.SMEM)
        vmem = pltpu.VMEM
        sem = pltpu.SemaphoreType.DMA
        found = pl.pallas_call(
            functools.partial(kernel, grid),
            out_shape=(shape, shape),
            in_specs=[hbm, hbm, smem, smem],
            out_specs=(hbm, hbm),
            scratch_shapes=[
                vmem((FACES, FACES, ROWS, ROWS), F32),
                vmem((FACES, ROWS, ROWS), F32),
                vmem((FACES, ROWS, HALF), F32),
                vmem((4, HALF + 8, HALF), F32),
                vmem((4, HALF + 8, HALF), F32),
                vmem((4, HALF, HALF), F32),
                vmem((4, HALF, HALF), F32),
                vmem((4, ROWS, HALF), F32),
                vmem((4, ROWS, HALF), F32),
                vmem((2, FACES, ROWS, HALF), F32),
                vmem((2, 4, ROWS, HALF), F32),
                vmem((2 * order, order), BF16),
                vmem((4, HALF, HALF), F32),
                vmem((2, HALF, HALF), F32),
                vmem((4, HALF, HALF), F32),
                vmem((2, HALF, HALF), F32),
                vmem((FACES, HALF, HALF), F32),
                vmem((FACES, 2 * ROWS, ROWS), BF16),
                vmem((FACES, ROWS, HALF), F32),
                vmem((order, ROWS), BF16),
                vmem((FACES, ROWS, HALF), F32),
                vmem((order, cases), F32),
                vmem((order, cases), F32),
                sem((12,)),
                sem((FACES, FACES)),
                sem((FACES,)),
                sem((FACES,)),
                sem((4,)),
                sem((4,)),
                sem((4,)),
                sem((4,)),
                sem((4,)),
                sem((4,)),
                sem((2, 4)),
                sem((2, 4)),
            ],
            compiler_params=pltpu.CompilerParams(
                collective_id=0, has_side_effects=True, vmem_limit_bytes=56 << 20),
        )(schur, loads, face_sizes, face_dir)
        return tuple(pl.pallas_call(
            hand_over,
            out_shape=(shape, shape),
            in_specs=[hbm, hbm],
            out_specs=(hbm, hbm),
            scratch_shapes=[vmem((2, 3, order // 3, cases), F32), sem((2, 2, 3))],
        )(*found))

    return jax.shard_map(
        local,
        mesh=mesh,
        in_specs=(
            P("wide", "depth", None, None),
            P("wide", "depth", None, None),
            P("wide", "depth", None),
            P("wide", "depth", None),
        ),
        out_specs=(P("wide", "depth", None, None), P("wide", "depth", None, None)),
        check_vma=False,
    )
```

time: 56.7 us -> 52.5 us (0.926)
  the two profiles are of different devices: /device:TPU:253 before, /device:TPU:22 now
where the time goes in v2:
time: 52.5 us; the launch traced here: 52.4 us
  Pallas kernels  51.8 us (99%)
  between operations  0.64 us (1%)
    pallas_call x1, Pallas kernels, local(): pl.pallas_call(functools.partial(kernel, grid), out_shape=(shape, shape),...  49.6 us
    pallas_call x1, Pallas kernels, local(): pl.pallas_call(hand_over, out_shape=(shape, shape), in_specs=[hbm, hbm],...  2.19 us

profile of v2, /device:TPU:22, one launch (start us, length us, event | category | flops | bytes accessed | tf_op | source)
XLA Modules:
  0.0 52.4 jit_solution(6865795757362727860)
XLA Ops:
  0.6 49.6 %shard_map.59 = (f32[1,1,1536,128]{3,2,1,0:T(8,128)}, f32[1,1,1536,128]{3,2,1,0:T(8,128)}) custom-call(f32[1,1,1536,1536]{3,2,1,0:T(8,128)} %schur.1, f32[1,1,1536,128]{3,2,1,0:T(8,128)} %loads.1, s32[1,1,6]{2,1,0:T(1,128)} %sizes.1, s32[1,1,6]{2,1,0:T(1,128)} %dirs.1), custom_call_target="tpu_custom_call" | custom-call | tf_op jit(solution)/shard_map/pallas_call | solution.py:428
  50.2 2.2 %shard_map.60 = (f32[1,1,1536,128]{3,2,1,0:T(8,128)}, f32[1,1,1536,128]{3,2,1,0:T(8,128)}) custom-call(f32[1,1,1536,128]{3,2,1,0:T(8,128)} %get-tuple-element.4.disp, f32[1,1,1536,128]{3,2,1,0:T(8,128)} %get-tuple-element.5.resid), custom_call_target="tpu_custom_call" | custom-call | tf_op jit(solution)/shard_map/pallas_call | solution.py:473

commit v3 on v2

--- a/solution.py
+++ b/solution.py
@@ -132,6 +132,69 @@
         fetch_diag.append(pltpu.make_async_copy(
             schur.at[0, 0, pl.ds(k * ROWS, ROWS), pl.ds(k * ROWS, ROWS)], diag.at[k], dma.at[k]))
         fetch_diag[-1].start()
+    barrier = pltpu.get_barrier_semaphore()
+    for i in range(4):
+        @pl.when(exists[i])
+        def _(i=i):
+            pl.semaphore_signal(barrier, inc=1, device_id=device[i], device_id_type=MESH)
+
+    def slot_of(direction):
+        k = jnp.int32(0)
+        for x in range(1, FACES):
+            k = jnp.where(dirs[0, 0, x] == direction, jnp.int32(x), k)
+        return k
+
+    slot = [slot_of(d) for d in ORDER]
+    size = []
+    for d in ORDER:
+        n = sizes[0, 0, 0]
+        for x in range(1, FACES):
+            n = jnp.where(dirs[0, 0, x] == d, sizes[0, 0, x], n)
+        size.append(n)
+
+    def remote(buffer, into, send, recv, i, index):
+        return pltpu.make_async_remote_copy(
+            src_ref=buffer.at[(*index, i)], dst_ref=into.at[(*index, i ^ 1)],
+            send_sem=send.at[(*index, i)], recv_sem=recv.at[(*index, i ^ 1)],
+            device_id=device[i], device_id_type=MESH)
+
+    def start(buffer, into, send, recv, i, index):
+        @pl.when(exists[i])
+        def _():
+            remote(buffer, into, send, recv, i, index).start()
+
+    def arrived(buffer, into, send, recv, i, index):
+        @pl.when(exists[i])
+        def _():
+            pltpu.make_async_remote_copy(
+                src_ref=buffer.at[(*index, i)], dst_ref=into.at[(*index, i)],
+                send_sem=send.at[(*index, i)], recv_sem=recv.at[(*index, i)],
+                device_id=device[i], device_id_type=MESH).wait_recv()
+
+    def sent(buffer, into, send, recv, i, index):
+        @pl.when(exists[i])
+        def _():
+            remote(buffer, into, send, recv, i, index).wait_send()
+
+    corners = (corner, got_corner, corner_s, corner_r)
+    pieces = (piece, got_piece, piece_s, piece_r)
+    firsts = (load_send, got_load, load_s, load_r)
+    faces = (face, got_face, face_s, face_r)
+
+    for i in range(4):
+        @pl.when(jnp.logical_not(exists[i]))
+        def _(i=i):
+            got_corner[i] = jnp.zeros((HALF + 8, HALF), F32)
+            got_piece[i] = jnp.zeros((HALF, HALF), F32)
+            got_load[i] = jnp.zeros((ROWS, HALF), F32)
+            for j in range(2):
+                got_face[j, i] = jnp.zeros((ROWS, HALF), F32)
+
+    for i in range(4, FACES):
+        got_face[1, i] = jnp.zeros((ROWS, HALF), F32)
+
+    for c in fetch_diag:
+        c.wait()
     fetch_load = []
     for k in range(FACES):
         fetch_load.append(pltpu.make_async_copy(
@@ -144,66 +207,6 @@
                 schur.at[0, 0, pl.ds(k * ROWS, ROWS), pl.ds(e * ROWS, ROWS)], full.at[k, e], full_s.at[k, e]))
             fetch_full[-1].start()
 
-    barrier = pltpu.get_barrier_semaphore()
-    for i in range(4):
-        @pl.when(exists[i])
-        def _(i=i):
-            pl.semaphore_signal(barrier, inc=1, device_id=device[i], device_id_type=MESH)
-
-    def slot_of(direction):
-        k = jnp.int32(0)
-        for x in range(1, FACES):
-            k = jnp.where(dirs[0, 0, x] == direction, jnp.int32(x), k)
-        return k
-
-    slot = [slot_of(d) for d in ORDER]
-    size = []
-    for d in ORDER:
-        n = sizes[0, 0, 0]
-        for x in range(1, FACES):
-            n = jnp.where(dirs[0, 0, x] == d, sizes[0, 0, x], n)
-        size.append(n)
-
-    def remote(buffer, into, send, recv, i, index):
-        return pltpu.make_async_remote_copy(
-            src_ref=buffer.at[(*index, i)], dst_ref=into.at[(*index, i ^ 1)],
-            send_sem=send.at[(*index, i)], recv_sem=recv.at[(*index, i ^ 1)],
-            device_id=device[i], device_id_type=MESH)
-
-    def start(buffer, into, send, recv, i, index):
-        @pl.when(exists[i])
-        def _():
-            remote(buffer, into, send, recv, i, index).start()
-
-    def arrived(buffer, into, send, recv, i, index):
-        @pl.when(exists[i])
-        def _():
-            pltpu.make_async_remote_copy(
-                src_ref=buffer.at[(*index, i)], dst_ref=into.at[(*index, i)],
-                send_sem=send.at[(*index, i)], recv_sem=recv.at[(*index, i)],
-                device_id=device[i], device_id_type=MESH).wait_recv()
-
-    def sent(buffer, into, send, recv, i, index):
-        @pl.when(exists[i])
-        def _():
-            remote(buffer, into, send, recv, i, index).wait_send()
-
-    corners = (corner, got_corner, corner_s, corner_r)
-    pieces = (piece, got_piece, piece_s, piece_r)
-    firsts = (load_send, got_load, load_s, load_r)
-    faces = (face, got_face, face_s, face_r)
-
-    for i in range(4):
-        @pl.when(jnp.logical_not(exists[i]))
-        def _(i=i):
-            got_corner[i] = jnp.zeros((HALF + 8, HALF), F32)
-            got_piece[i] = jnp.zeros((HALF, HALF), F32)
-            got_load[i] = jnp.zeros((ROWS, HALF), F32)
-            for j in range(2):
-                got_face[j, i] = jnp.zeros((ROWS, HALF), F32)
-
-    for c in fetch_diag:
-        c.wait()
     hr = lax.broadcasted_iota(jnp.int32, (HALF, HALF), 0)
     hc = lax.broadcasted_iota(jnp.int32, (HALF, HALF), 1)
     parts = ((0, 0), (HALF, 0), (HALF, HALF))
@@ -223,7 +226,7 @@
     for e in exists:
         count = count + jnp.where(e, jnp.int32(1), jnp.int32(0))
     pl.semaphore_wait(barrier, count)
-    for i in range(4):
+    for i in (2, 3, 0, 1):
         start(*corners, i, ())
     for c in fetch_load:
         c.wait()
@@ -285,10 +288,10 @@
         c.wait()
     for i in (4, 5, 2, 3, 0, 1):
         at(top, i)[...] = rotate(assembled(0, i), i)
-    for i in range(4):
+    for i in (2, 3, 0, 1):
         start(*pieces, i, ())
 
-    for i in range(4):
+    for i in (2, 3, 0, 1):
         start(*firsts, i, ())
 
     def beside_top(s):
@@ -361,7 +364,7 @@
     for i in (0, 1):
         arrived(*faces, i, (0,))
         keep(i, u[i] + solve(i, face[0, i] + got_face[0, i]))
-    for i in range(0, FACES, 2):
+    for i in (2, 0, 4):
         for j, x in enumerate(applied(i, 0, 2)):
             face[1, i + j] = acc[i + j] - x
             if i < 4:
@@ -381,14 +384,10 @@
 
     for k in range(FACES):
         give(k, u[place(k)], out_disp, disp_out, disp_s)
-    for i in (4, 5, 2, 3, 0, 1):
-        x = face[1, i]
-        if i < 4:
-            arrived(*faces, i, (1,))
-            x = x + got_face[1, i]
-        acc[i] = x
+    for i in range(4):
+        arrived(*faces, i, (1,))
     for k in range(FACES):
-        give(k, acc[place(k)], out_resid, resid_out, resid_s)
+        give(k, face[1, place(k)] + got_face[1, place(k)], out_resid, resid_out, resid_s)
     for i in range(4):
         sent(*corners, i, ())
         sent(*pieces, i, ())
@@ -441,7 +440,7 @@
                 vmem((4, ROWS, HALF), F32),
                 vmem((4, ROWS, HALF), F32),
                 vmem((2, FACES, ROWS, HALF), F32),
-                vmem((2, 4, ROWS, HALF), F32),
+                vmem((2, FACES, ROWS, HALF), F32),
                 vmem((2 * order, order), BF16),
                 vmem((4, HALF, HALF), F32),
                 vmem((2, HALF, HALF), F32),

time: 52.5 us -> 51.9 us (0.989)
  the two profiles are of different devices: /device:TPU:22 before, /device:TPU:28 now
where the time goes in v3:
time: 51.9 us; the launch traced here: 51.8 us
  Pallas kernels  51.1 us (98%)
  between operations  0.64 us (1%)
    pallas_call x1, Pallas kernels, local(): pl.pallas_call(functools.partial(kernel, grid), out_shape=(shape, shape),...  48.9 us
    pallas_call x1, Pallas kernels, local(): pl.pallas_call(hand_over, out_shape=(shape, shape), in_specs=[hbm, hbm],...  2.19 us

profile of v3, /device:TPU:28, one launch (start us, length us, event | category | flops | bytes accessed | tf_op | source)
XLA Modules:
  0.0 51.8 jit_solution(934899766359865328)
XLA Ops:
  0.6 48.9 %shard_map.59 = (f32[1,1,1536,128]{3,2,1,0:T(8,128)}, f32[1,1,1536,128]{3,2,1,0:T(8,128)}) custom-call(f32[1,1,1536,1536]{3,2,1,0:T(8,128)} %schur.1, f32[1,1,1536,128]{3,2,1,0:T(8,128)} %loads.1, s32[1,1,6]{2,1,0:T(1,128)} %sizes.1, s32[1,1,6]{2,1,0:T(1,128)} %dirs.1), custom_call_target="tpu_custom_call" | custom-call | tf_op jit(solution)/shard_map/pallas_call | solution.py:427
  49.6 2.2 %shard_map.60 = (f32[1,1,1536,128]{3,2,1,0:T(8,128)}, f32[1,1,1536,128]{3,2,1,0:T(8,128)}) custom-call(f32[1,1,1536,128]{3,2,1,0:T(8,128)} %get-tuple-element.4.disp, f32[1,1,1536,128]{3,2,1,0:T(8,128)} %get-tuple-element.5.resid), custom_call_target="tpu_custom_call" | custom-call | tf_op jit(solution)/shard_map/pallas_call | solution.py:472
